TPU v7x, 256 devices: a whole 4x4x8 slice. The times are simulated.
256 devices in a mesh: owner: 16 (over y, x), split: 16 (over z, core).
Axes of the slice: x: 4, y: 4, z: 8, core: 2. Of those that a mesh axis runs over, the one named last changes fastest.
Arguments:
- embeddings: bfloat16 [131072, 1024], P(('owner', 'split'))
- cluster_id: int32 [131072], P(('owner', 'split')), may hold values from 0 to 4095, as said below
- doc_order: int32 [131072], P(('owner', 'split')), may hold values from 0 to 131071, each once
Outputs:
- best_similarity: float32 [131072], P(('owner', 'split'))
Inputs may be any that keep to these rules, and one draw needn't show every extreme that they name: `cluster_id`: cluster c belongs to the device with owner index c mod 16 and split index (c // 16) mod 16. Of the rows of one device at most 4 belong to clusters of any one device, and in every draw some device gets exactly 4 rows from every device. The rows of one device hold at most one document of each cluster.
All inputs are finite; a program needn't handle non-finite values.
Results may differ from a plain program's by a relative error of at most 0.00046.
Values may be sent and summed in bfloat16 or wider, within the bound.
A program may use at most 128 MiB of HBM per device.

v0:
```python
import math

import jax
import jax.numpy as jnp
from jax import lax
from jax.sharding import PartitionSpec as P


def local(embeddings, cluster_id, doc_order):
    row_count, feat_width = embeddings.shape
    owner_count = lax.axis_size("owner")
    split_count = lax.axis_size("split")
    device_count = owner_count * split_count
    capacity = 2 * row_count // device_count
    values = embeddings.astype(jnp.float32)
    unit_rows = (
        values * lax.rsqrt(jnp.sum(values * values, axis=1, keepdims=True) + 1e-06)
    ).astype(jnp.bfloat16)
    target = cluster_id % owner_count * split_count + cluster_id // owner_count % split_count
    onehot = (target[:, None] == jnp.arange(device_count, dtype=jnp.int32)[None, :]).astype(
        jnp.int32
    )
    ranking = jnp.sum((jnp.cumsum(onehot, axis=0) - onehot) * onehot, axis=1)
    slot_index = target * capacity + ranking
    slot_total = device_count * capacity
    send_unit = jnp.zeros((slot_total, feat_width), jnp.bfloat16).at[slot_index].set(unit_rows)
    send_cluster = jnp.full((slot_total,), -1, jnp.int32).at[slot_index].set(cluster_id)
    send_order = jnp.zeros((slot_total,), jnp.int32).at[slot_index].set(doc_order)
    packed = (
        send_unit.reshape(owner_count, split_count, capacity, feat_width),
        send_cluster.reshape(owner_count, split_count, capacity),
        send_order.reshape(owner_count, split_count, capacity),
    )
    first_unit, first_cluster, first_order = (
        lax.all_to_all(packed[0], "owner", split_axis=0, concat_axis=0, tiled=True),
        lax.all_to_all(packed[1], "owner", split_axis=0, concat_axis=0, tiled=True),
        lax.all_to_all(packed[2], "owner", split_axis=0, concat_axis=0, tiled=True),
    )
    wide_unit, wide_cluster, wide_order = (
        lax.all_gather(first_unit[None], "split", axis=0, tiled=True),
        lax.all_gather(first_cluster[None], "split", axis=0, tiled=True),
        lax.all_gather(first_order[None], "split", axis=0, tiled=True),
    )
    position = lax.axis_index("split")
    got_unit = jnp.swapaxes(
        lax.dynamic_index_in_dim(wide_unit, position, axis=2, keepdims=False), 0, 1
    )
    got_cluster = jnp.swapaxes(
        lax.dynamic_index_in_dim(wide_cluster, position, axis=2, keepdims=False), 0, 1
    )
    got_order = jnp.swapaxes(
        lax.dynamic_index_in_dim(wide_order, position, axis=2, keepdims=False), 0, 1
    )
    query_unit = got_unit.reshape(slot_total, feat_width)
    query_cluster = got_cluster.reshape(slot_total)
    query_order = got_order.reshape(slot_total)
    sort_cluster = jnp.where(query_cluster >= 0, query_cluster, jnp.int32(2**30))
    by_order = jnp.argsort(query_order, stable=True)
    by_cluster = jnp.argsort(sort_cluster[by_order], stable=True)
    sorting = by_order[by_cluster]
    sorted_unit = jnp.concatenate(
        [jnp.zeros((device_count, feat_width), jnp.bfloat16), query_unit[sorting]], axis=0
    )
    sorted_cluster = jnp.concatenate(
        [jnp.full((device_count,), -1, jnp.int32), query_cluster[sorting]], axis=0
    )
    sorted_order = jnp.concatenate(
        [jnp.zeros((device_count,), jnp.int32), query_order[sorting]], axis=0
    )
    block_rows = math.gcd(slot_total, 512)
    results = []
    for block in range(slot_total // block_rows):
        start = block * block_rows
        queries = sorted_unit[start + device_count : start + device_count + block_rows]
        own_cluster = sorted_cluster[start + device_count : start + device_count + block_rows]
        own_order = sorted_order[start + device_count : start + device_count + block_rows]
        keys = sorted_unit[start : start + device_count + block_rows]
        key_cluster = sorted_cluster[start : start + device_count + block_rows]
        key_order = sorted_order[start : start + device_count + block_rows]
        scores = lax.dot_general(
            queries, keys, (((1,), (1,)), ((), ())), preferred_element_type=jnp.float32
        )
        admitted = (
            (own_cluster[:, None] == key_cluster[None, :])
            & (own_cluster[:, None] >= 0)
            & (key_order[None, :] < own_order[:, None])
        )
        results.append(jnp.max(jnp.where(admitted, scores, -1.0), axis=1))
    highest_sorted = jnp.concatenate(results, axis=0)
    highest = jnp.zeros((slot_total,), jnp.float32).at[sorting].set(highest_sorted)
    answers = lax.all_to_all(
        lax.all_to_all(
            highest.reshape(owner_count, split_count, capacity),
            "owner",
            split_axis=0,
            concat_axis=0,
            tiled=True,
        ),
        "split",
        split_axis=1,
        concat_axis=1,
        tiled=True,
    )
    return answers.reshape(slot_total)[slot_index]


def solution(mesh):
    in_specs = (P(("owner", "split"), None), P(("owner", "split")), P(("owner", "split")))
    out_specs = P(("owner", "split"))
    return jax.shard_map(local, mesh=mesh, in_specs=in_specs, out_specs=out_specs, check_vma=False)
```

profile of v0, /device:TPU:1, one launch (start us, length us, event | category | flops | bytes accessed | tf_op | source)
XLA Modules:
  0.0 300.1 jit_solution(12001172596881248557)
XLA Ops:
  6.5 0.8 fusion.34
  7.3 0.7 fusion.21
  8.1 0.2 fusion.15
  8.6 0.2 fusion.14
  8.8 0.3 fusion
  9.1 3.3 %scatter_custom_fusion.2 = bf16[1024,1024]{1,0:T(8,128)(2,1)S(1)} fusion(s32[512]{0:T(512)S(1)} %compare_select_fusion.4, bf16[512,1024]{1,0:T(8,128)(2,1)S(1)} %copy-done, f32[512]{0:T(512)S(1)} %add_rsqrt_fusion, bf16[]{:T(256)} %constant.73.clone.1), kind=kCustom, calls=%fused_computation.21 | custom fusion | flops 1572864 | bytes 3147778 | tf_op jit(solution)/shard_map/scatter | solution.py:26
  12.4 2.2 reshape.76
  14.7 2.4 copy.22
  17.0 34.9 %all_to_all.25 = bf16[16,16,4,1024]{3,1,2,0:T(8,128)(2,1)} all-to-all(bf16[16,16,4,1024]{3,1,2,0:T(8,128)(2,1)S(1)} %copy.22), channel_id=1, replica_groups=mesh['owner'=16,'split'=16] {'owner'}, dimensions={0} | all-to-all | bytes 4194304 | tf_op jit(solution)/shard_map/all_to_all | solution.py:35
  51.9 2.4 scatter_custom_fusion.1
  54.4 0.1 reshape.74
  54.5 0.8 copy.20
  55.3 3.5 %all-to-all-start.1 = ((s32[16,16,4]{1,2,0:T(4,128)}), s32[16,16,4]{1,2,0:T(4,128)S(1)}, u32[]{:S(2)}, u32[]{:S(2)}) async-start(s32[16,16,4]{1,2,0:T(4,128)} %copy.20), calls=%async_computation.1 | async-start | bytes 65536 | tf_op jit(solution)/shard_map/all_to_all | solution.py:36
  58.8 2.6 scatter_custom_fusion
  61.4 0.1 reshape.72
  61.5 0.8 copy.18
  62.3 2.9 all-to-all-done.1
  65.1 3.7 %all-to-all-start = ((s32[16,16,4]{1,2,0:T(4,128)}), s32[16,16,4]{1,2,0:T(4,128)S(1)}, u32[]{:S(2)}, u32[]{:S(2)}) async-start(s32[16,16,4]{1,2,0:T(4,128)} %copy.18), calls=%async_computation | async-start | bytes 65536 | tf_op jit(solution)/shard_map/all_to_all | solution.py:37
  68.9 26.8 %all-gather.1 = s32[256,16,4]{1,2,0:T(4,128)S(1)} all-gather(s32[16,16,4]{1,2,0:T(4,128)S(1)} %all-to-all-done.1), channel_id=3, replica_groups=mesh['owner'=16,'split'=16] {'split'}, dimensions={0}, use_global_device_ids=true | all-gather | bytes 69632 | tf_op jit(solution)/shard_map/all_gather | solution.py:41
  95.7 18.8 %all-gather = s32[256,16,4]{1,2,0:T(4,128)S(1)} all-gather(s32[16,16,4]{1,2,0:T(4,128)S(1)} %all-to-all-done), channel_id=2, replica_groups=mesh['owner'=16,'split'=16] {'split'}, dimensions={0}, use_global_device_ids=true | all-gather | bytes 69632 | tf_op jit(solution)/shard_map/all_gather | solution.py:42
  114.4 0.6 constant_dynamic-slice_fusion
  115.1 1.6 copy.19
  116.7 0.1 reshape.73
  116.8 1.6 copy.21
  118.4 0.1 reshape.75
  118.6 4.4 %sort.31 = (s32[1024]{0:T(1024)}, s32[1024]{0:T(1024)S(1)}) sort(s32[1024]{0:T(1024)S(1)} %reshape.73, s32[1024]{0:T(1024)S(1)} %iota.15), dimensions={0}, to_apply=%region_4.5 | sort | flops 10240 | bytes 16384 | tf_op jit(solution)/shard_map/jit(argsort)/sort | solution.py:58
  122.9 4.7 %gather_fusion = s32[1024]{0:T(1024)S(1)} fusion(s32[1024]{0:T(1024)S(1)} %compare_select_fusion.3, s32[1024]{0:T(1024)S(1)} %fusion.18), kind=kCustom, calls=%fused_computation | custom fusion | bytes 12288 | tf_op jit(solution)/shard_map/gather | solution.py:59
  127.7 4.4 %sort.32 = (s32[1024]{0:T(1024)}, s32[1024]{0:T(1024)S(1)}) sort(s32[1024]{0:T(1024)S(1)} %gather_fusion, s32[1024]{0:T(1024)S(1)} %iota.16), dimensions={0}, to_apply=%region_6.7 | sort | flops 10240 | bytes 16384 | tf_op jit(solution)/shard_map/jit(argsort)/sort | solution.py:59
  132.0 4.5 %gather_fusion.1 = s32[1024]{0:T(1024)S(1)} fusion(s32[1024]{0:T(1024)S(1)} %get-tuple-element.7, s32[1024]{0:T(1024)S(1)} %fusion.19), kind=kCustom, calls=%fused_computation.1 | custom fusion | bytes 12288 | tf_op jit(solution)/shard_map/gather | solution.py:60
  136.6 4.5 %gather_fusion.3 = s32[1024]{0:T(1024)S(1)} fusion(s32[1024]{0:T(1024)S(1)} %reshape.73, s32[1024]{0:T(1024)S(1)} %broadcast_clamp_fusion), kind=kCustom, calls=%fused_computation.3 | custom fusion | bytes 12288 | tf_op jit(solution)/shard_map/gather | solution.py:68
  141.1 4.5 %gather_fusion.2 = s32[1024]{0:T(1024)S(1)} fusion(s32[1024]{0:T(1024)S(1)} %reshape.75, s32[1024]{0:T(1024)S(1)} %broadcast_clamp_fusion), kind=kCustom, calls=%fused_computation.2 | custom fusion | bytes 12288 | tf_op jit(solution)/shard_map/gather | solution.py:65
  145.7 87.2 %all-gather.5.cloned.1.call-done = bf16[256,16,4,1024]{3,1,2,0:T(8,128)(2,1)} async-done(((bf16[16,16,4,1024]{3,1,2,0:T(8,128)(2,1)}), bf16[256,16,4,1024]{3,1,2,0:T(8,128)(2,1)}) %all-gather.5.cloned.1.call-update) | async-done | bytes 33554448 | tf_op jit(solution)/shard_map/all_gather | solution.py:40
  232.9 7.7 %constant_dynamic-slice_fusion.2 = bf16[16,16,1,4,1024]{4,2,3,1,0:T(2,128)(2,1)S(1)} fusion(bf16[16,16,16,4,1024]{4,2,3,1,0:T(8,128)(2,1)} %bitcast.38, s32[]{:T(128)S(6)} %select_n.63), kind=kLoop, calls=%fused_computation.73 | loop fusion | bytes 4194308 | tf_op jit(solution)/shard_map/jit(dynamic_index_in_dim)/dynamic_slice | solution.py:46
  240.6 2.3 copy.29
  242.9 3.0 copy.24
  245.9 2.5 reshape.77
  248.4 5.4 %gather_fusion.4 = bf16[1024,1024]{1,0:T(8,128)(2,1)} fusion(bf16[1024,1024]{1,0:T(8,128)(2,1)S(1)} %reshape.77, s32[1024]{0:T(1024)S(1)} %broadcast_clamp_fusion), kind=kCustom, calls=%fused_computation.4 | custom fusion | bytes 4198400 | tf_op jit(solution)/shard_map/gather | solution.py:62
  253.8 3.1 %select_reduce_fusion = f32[512]{0:T(512)S(1)} fusion(bf16[1024,1024]{1,0:T(8,128)(2,1)} %gather_fusion.4, s32[768]{0:T(1024)S(1)} %get-tuple-element.18, s32[768]{0:T(1024)S(1)} %get-tuple-element.16, s32[512]{0:T(512)S(1)} %get-tuple-element.14, s32[512]{0:T(512)S(1)} %get-tuple-element.12, pred[512]{0:T(512)(128)(4,1)S(1)} %get-tuple-element.10), kind=kOutput, calls=%fused_computation.19 | convolution fusion | flops 807665152 | bytes 2634240 | tf_op jit(solution)/shard_map/dot_general | solution.py:80
  256.9 1.2 select_reduce_fusion.1
  258.1 4.3 %scatter_custom_fusion.3 = f32[1024]{0:T(1024)S(1)} fusion(s32[1024]{0:T(1024)S(1)} %bitcast.41, f32[1024]{0:T(1024)S(1)} %pad_maximum_fusion, f32[]{:T(128)} %constant.39.clone.1), kind=kCustom, calls=%fused_computation.65 | custom fusion | bytes 4100 | tf_op jit(solution)/shard_map/scatter | solution.py:90
  262.4 0.1 reshape.78
  262.6 0.2 copy.25
  262.7 12.8 %all_to_all.26 = f32[16,16,4]{1,2,0:T(4,128)S(1)} all-to-all(f32[16,16,4]{1,2,0:T(4,128)S(1)} %copy.25), channel_id=1, replica_groups=mesh['owner'=16,'split'=16] {'owner'}, dimensions={0} | all-to-all | bytes 8192 | tf_op jit(solution)/shard_map/all_to_all | solution.py:92
  275.5 0.7 copy.26
  276.2 6.0 %all-to-all-start.4 = ((f32[16,16,4]{0,2,1:T(4,128)}), f32[16,16,4]{0,2,1:T(4,128)S(1)}, u32[]{:S(2)}, u32[]{:S(2)}) async-start(f32[16,16,4]{0,2,1:T(4,128)} %copy.26), calls=%async_computation.4 | async-start | bytes 65536 | tf_op jit(solution)/shard_map/all_to_all | solution.py:91
  282.2 7.4 %all-to-all-done.4 = f32[16,16,4]{0,2,1:T(4,128)S(1)} async-done(((f32[16,16,4]{0,2,1:T(4,128)}), f32[16,16,4]{0,2,1:T(4,128)S(1)}, u32[]{:S(2)}, u32[]{:S(2)}) %all-to-all-start.4) | async-done | bytes 4128 | tf_op jit(solution)/shard_map/all_to_all | solution.py:91
  289.6 0.2 copy.27
  289.9 3.4 %gather_fusion.5 = f32[512]{0:T(512)} fusion(f32[1024]{0:T(1024)S(1)} %reshape.79, s32[1024]{0:T(1024)S(1)} %pad_clamp_fusion), kind=kCustom, calls=%fused_computation.5 | custom fusion | bytes 6144 | tf_op jit(solution)/shard_map/gather | solution.py:104
  (33 shorter events, 0.6 us)
Async XLA Ops:
  6.5 2.3 copy-start.2
  6.5 2.3 copy-start
  6.5 226.4 %all-gather.5.cloned.1.call-start = ((), (), s32[]{:S(2)}) async-start(), calls=%async_computation.5 | async-start | bytes 35651584 | tf_op jit(solution)/shard_map/all_gather | solution.py:40
  55.3 9.9 %all-to-all-start.1 = ((s32[16,16,4]{1,2,0:T(4,128)}), s32[16,16,4]{1,2,0:T(4,128)S(1)}, u32[]{:S(2)}, u32[]{:S(2)}) async-start(s32[16,16,4]{1,2,0:T(4,128)} %copy.20), calls=%async_computation.1 | async-start | bytes 65536 | tf_op jit(solution)/shard_map/all_to_all | solution.py:36
  65.1 30.5 %all-to-all-start = ((s32[16,16,4]{1,2,0:T(4,128)}), s32[16,16,4]{1,2,0:T(4,128)S(1)}, u32[]{:S(2)}, u32[]{:S(2)}) async-start(s32[16,16,4]{1,2,0:T(4,128)} %copy.18), calls=%async_computation | async-start | bytes 65536 | tf_op jit(solution)/shard_map/all_to_all | solution.py:37
  253.8 3.1 %copy-start.1 = (bf16[1024,1024]{1,0:T(8,128)(2,1)S(1)}, bf16[1024,1024]{1,0:T(8,128)(2,1)}, u32[]{:S(2)}) copy-start(bf16[1024,1024]{1,0:T(8,128)(2,1)} %gather_fusion.4) | copy-start | bytes 6291460
  276.2 13.4 %all-to-all-start.4 = ((f32[16,16,4]{0,2,1:T(4,128)}), f32[16,16,4]{0,2,1:T(4,128)S(1)}, u32[]{:S(2)}, u32[]{:S(2)}) async-start(f32[16,16,4]{0,2,1:T(4,128)} %copy.26), calls=%async_computation.4 | async-start | bytes 65536 | tf_op jit(solution)/shard_map/all_to_all | solution.py:91
Sparse Core Ops, SparseCore 0:
  52.0 180.8 all-gather.4
where the time goes:
time: 301 us; the launch traced here: 300 us
  waiting for transfers between devices  97.5 us (32%)
  blocking collectives  93.2 us (31%)
  local copies, waits for them, and re-layouts  64 us (21%)
  other arithmetic  14.4 us (5%)
  between operations  13.7 us (5%)
  starting transfers between devices  13.2 us (4%)
  matrix products  4.29 us (1%)
    all_gather x1, waiting for transfers between devices, local(): lax.all_gather(first_unit[None], 'split', axis=0, tiled=True)  87.2 us
    all_to_all x1, blocking collectives, local(): lax.all_to_all(packed[0], 'owner', split_axis=0, concat_axis=0, tiled=True)  34.9 us
    all_gather x1, blocking collectives, local(): lax.all_gather(first_cluster[None], 'split', axis=0, tiled=True)  26.8 us
    all_gather x1, blocking collectives, local(): lax.all_gather(first_order[None], 'split', axis=0, tiled=True)  18.8 us
    all_to_all x1, blocking collectives, local(): lax.all_to_all(highest.reshape(owner_count, split_count, capacity), 'owne...  12.8 us
    dynamic_slice x2, local copies, waits for them, and re-layouts, local(): lax.dynamic_index_in_dim(wide_unit, position, axis=2, keepdims=False)  10 us
    all_to_all x1, waiting for transfers between devices, local(): lax.all_to_all(lax.all_to_all(highest.reshape(owner_count, split_count, c...  7.38 us
  transfers between devices with their start and end apart: 4, of which 3 were waited for; matrix products, arithmetic and copies ran while one was open for 13% of the time, Pallas kernels for 0%

commit v1 on v0

v1 whole, which is shorter than its diff:
```python
import jax
import jax.numpy as jnp
from jax import lax
from jax.experimental import pallas as pl
from jax.experimental.pallas import tpu as pltpu
from jax.sharding import PartitionSpec as P

MESH = pl.DeviceIdType.MESH
F32 = jnp.float32
BF16 = jnp.bfloat16

NY, NX, NZ, NC = 4, 4, 8, 2
NO, NS = NY * NX, NZ * NC
CAP = 4
ROWS = 512
DIM = 1024
QUART = DIM // 4
SLOTS = NO * NS * CAP
UNIT = NS * CAP
SLAB = 16
BLOCK = NS * SLAB


def iota(shape, dim):
    return lax.broadcasted_iota(jnp.int32, shape, dim)


def dot(a, b, contract):
    return lax.dot_general(a, b, ((contract[:1], contract[1:]), ((), ())), preferred_element_type=F32)


def kernel(
    emb_ref, clu_ref, ord_ref, out_ref,
    unit, onehot, slot, send, recv, keys, meta_out, meta_mid, meta_in, meta_col,
    best_col, best_row, ans_out, ans_mid, ans_in,
    send_sem, recv_sem, ma_s, ma_r, mb_s, mb_r, aa_s, aa_r, ab_s, ab_r, ready,
):
    me_o = lax.axis_index("owner")
    me_s = lax.axis_index("split")
    y, x = me_o // NX, lax.rem(me_o, NX)
    z, c = me_s // NC, lax.rem(me_s, NC)

    def owner_at(k, sign=1):
        dy, dx = k // NX, k % NX
        if sign < 0:
            dy, dx = NY - dy, NX - dx
        return lax.rem(y + dy, NY) * NX + lax.rem(x + dx, NX)

    def split_at(k, sign=1):
        dz, dc = k // NC, k % NC
        if sign < 0:
            dz = NZ - dz
        return lax.rem(z + dz, NZ) * NC + lax.rem(c + dc, NC)

    def remote(src, dst, ssem, rsem, device):
        return pltpu.make_async_remote_copy(
            src_ref=src, dst_ref=dst, send_sem=ssem, recv_sem=rsem,
            device_id=device, device_id_type=MESH,
        )

    barrier = pltpu.get_barrier_semaphore()
    for k in range(1, NS):
        pl.semaphore_signal(barrier, inc=1, device_id=(me_o, split_at(k)), device_id_type=MESH)
    for k in range(1, NO):
        pl.semaphore_signal(barrier, inc=1, device_id=(owner_at(k), me_s), device_id_type=MESH)

    clu = clu_ref[...]
    orders = ord_ref[...]
    to_o = clu & (NO - 1)
    to_s = (clu >> 4) & (NS - 1)
    rel_y = ((to_o >> 2) - y) & (NY - 1)
    rel_x = ((to_o & (NX - 1)) - x) & (NX - 1)
    rel_z = ((to_s >> 1) - z) & (NZ - 1)
    rel_c = ((to_s & 1) - c) & 1
    k_o = rel_y * NX + rel_x
    k_s = rel_z * NC + rel_c
    goal = k_o * NS + k_s
    hot = (goal == iota((NO * NS, ROWS), 0)).astype(F32)
    onehot[...] = hot.astype(BF16)
    before = (iota((ROWS, ROWS), 0) < iota((ROWS, ROWS), 1)).astype(F32).astype(BF16)
    count = dot(onehot[...], before, (1, 0))
    rank = jnp.sum(hot * count, axis=0, keepdims=True).astype(jnp.int32)
    slot[...] = k_o * UNIT + rank * NS + k_s

    line = iota((8, ROWS), 0)
    code = clu + 1
    parts = jnp.where(
        line == 0, orders >> 12,
        jnp.where(line == 1, (orders >> 6) & 63,
                  jnp.where(line == 2, orders & 63,
                            jnp.where(line == 3, code >> 6,
                                      jnp.where(line == 4, code & 63, 0)))),
    ).astype(F32).astype(BF16)
    by_split = k_s * UNIT + k_o * CAP + rank
    pick = (by_split == iota((SLOTS, ROWS), 0)).astype(F32).astype(BF16)
    got = dot(parts, pick, (1, 1))
    slot_order = got[0:1] * 4096.0 + got[1:2] * 64.0 + got[2:3]
    slot_cluster = got[3:4] * 64.0 + got[4:5] - 1.0
    low = iota((1, 128), 1) < 64
    for p in range(NS // 2):
        a = slot_order[:, p * 128 : (p + 1) * 128]
        b = slot_cluster[:, p * 128 : (p + 1) * 128]
        meta_out[2 * p] = jnp.where(low, a, pltpu.roll(b, 64, 1))
        meta_out[2 * p + 1] = jnp.where(low, pltpu.roll(a, 64, 1), b)

    values = emb_ref[...].astype(F32)
    scale = lax.rsqrt(jnp.sum(values * values, axis=1, keepdims=True) + 1e-06)
    unit[...] = (values * scale).astype(BF16)

    pl.semaphore_wait(barrier, NS - 1 + NO - 1)
    for k in range(1, NO):
        pl.semaphore_signal(ready, inc=1, device_id=(owner_at(k), me_s), device_id_type=MESH)
    for k in range(1, NS):
        remote(meta_out.at[k], meta_mid.at[k], ma_s, ma_r, (me_o, split_at(k))).start()
    meta_mid[0] = meta_out[0]
    pl.semaphore_wait(ready, NO - 1)

    row, col = iota((BLOCK, BLOCK), 0), iota((BLOCK, BLOCK), 1)
    weave = (
        col == ((row >> 2) & 3) * UNIT + (row & 3) * NS + (row >> 4)
    ).astype(F32).astype(BF16)
    unweave = (
        row == ((col >> 2) & 3) * UNIT + (col & 3) * NS + (col >> 4)
    ).astype(F32).astype(BF16)

    for b in range(NO):
        choose = (slot[...] == b * UNIT + iota((UNIT, ROWS), 0)).astype(F32).astype(BF16)
        rows = dot(choose, unit[...], (1, 0)).astype(BF16)
        quarters = jnp.concatenate([rows[:, q * QUART : (q + 1) * QUART] for q in range(4)], axis=0)
        send[b * BLOCK : (b + 1) * BLOCK] = dot(weave, quarters, (1, 0)).astype(BF16)
        for k in range(NS):
            part = pl.ds(b * BLOCK + k * SLAB, SLAB)
            if b == 0 and k == 0:
                recv[part] = send[part]
                continue
            remote(
                send.at[part], recv.at[part], send_sem.at[b], recv_sem.at[b],
                (owner_at(b), split_at(k)),
            ).start()

    some = remote(meta_out.at[pl.ds(1, NS - 1)], meta_mid.at[pl.ds(1, NS - 1)], ma_s, ma_r, (me_o, split_at(1)))
    some.wait_recv()
    for k in range(1, NO):
        remote(meta_mid, meta_in.at[k], mb_s, mb_r, (owner_at(k), me_s)).start()
    meta_in[0] = meta_mid[...]
    some.wait_send()
    many = remote(meta_in.at[pl.ds(1, NO - 1)], meta_in.at[pl.ds(1, NO - 1)], mb_s, mb_r, (owner_at(1), me_s))
    many.wait_recv()
    for b in range(NO):
        lines = meta_in[b].reshape(NS, 128)
        for r in range(CAP):
            at = b * UNIT + r * NS
            lane = b * CAP + r
            meta_col[at : at + NS] = pltpu.roll(lines, 128 - lane, 1) if lane else lines
    many.wait_send()
    turned = meta_col[...].T
    row_order, row_cluster = turned[0:1], turned[64:65]

    best_row[...] = jnp.full((1, SLOTS), -1.0, F32)
    step = 2
    for g in range(0, NO, step):
        for b in range(g, g + step):
            first = SLAB if b == 0 else 0
            span = pl.ds(b * BLOCK + first, BLOCK - first)
            remote(
                send.at[span], recv.at[span], send_sem.at[b], recv_sem.at[b], (me_o, split_at(1))
            ).wait_recv()
            woven = dot(unweave, recv[b * BLOCK : (b + 1) * BLOCK], (1, 0)).astype(BF16)
            for q in range(4):
                keys[b * UNIT : (b + 1) * UNIT, q * QUART : (q + 1) * QUART] = woven[
                    q * UNIT : (q + 1) * UNIT
                ]
        lo, hi = g * UNIT, (g + step) * UNIT
        score = dot(keys[lo:hi], keys[0:hi], (1, 1))
        new_order, new_cluster = meta_col[lo:hi, 0:1], meta_col[lo:hi, 64:65]
        old_order, old_cluster = row_order[:, :hi], row_cluster[:, :hi]
        score = jnp.where(new_cluster == old_cluster, score, -1.0)
        best = jnp.max(jnp.where(old_order < new_order, score, -1.0), axis=1, keepdims=True)
        best_col[lo:hi] = jnp.broadcast_to(best, (hi - lo, 128))
        best = jnp.max(jnp.where(new_order < old_order, score, -1.0), axis=0, keepdims=True)
        best_row[:, :hi] = jnp.maximum(best_row[:, :hi], best)

    final = jnp.maximum(best_col[...], jnp.broadcast_to(best_row[...], (128, SLOTS)).T)
    lanes = iota((NS, 128), 1)
    answer = jnp.zeros((NS, 128), F32)
    for u in range(UNIT):
        answer = jnp.where(lanes == u, final[u * NS : (u + 1) * NS], answer)
    ans_out[...] = answer.reshape(NS, 1, 128)
    for k in range(1, NS):
        remote(ans_out.at[k], ans_mid.at[k], aa_s, aa_r, (me_o, split_at(k, -1))).start()
    ans_mid[0] = ans_out[0]
    some = remote(ans_out.at[pl.ds(1, NS - 1)], ans_mid.at[pl.ds(1, NS - 1)], aa_s, aa_r, (me_o, split_at(1)))
    some.wait_recv()
    for k in range(1, NO):
        remote(ans_mid, ans_in.at[k], ab_s, ab_r, (owner_at(k, -1), me_s)).start()
    ans_in[0] = ans_mid[...]
    some.wait_send()
    many = remote(ans_in.at[pl.ds(1, NO - 1)], ans_in.at[pl.ds(1, NO - 1)], ab_s, ab_r, (owner_at(1), me_s))
    many.wait_recv()

    table = ans_in[...].reshape(NO * NS, 128).T
    high = table.astype(BF16)
    rest = table - high.astype(F32)
    mid = rest.astype(BF16)
    tiny = (rest - mid.astype(F32)).astype(BF16)
    mine = dot(high, onehot[...], (1, 0)) + dot(mid, onehot[...], (1, 0)) + dot(tiny, onehot[...], (1, 0))
    place = k_o * CAP + rank
    out_ref[...] = jnp.sum(jnp.where(iota((128, ROWS), 0) == place, mine, 0.0), axis=0, keepdims=True)

    many.wait_send()
    for b in range(NO):
        first = SLAB if b == 0 else 0
        span = pl.ds(b * BLOCK + first, BLOCK - first)
        remote(
            send.at[span], recv.at[span], send_sem.at[b], recv_sem.at[b], (me_o, split_at(1))
        ).wait_send()


def local(embeddings, cluster_id, doc_order):
    vmem = pl.BlockSpec(memory_space=pltpu.VMEM)
    dma = pltpu.SemaphoreType.DMA
    out = pl.pallas_call(
        kernel,
        name="dedup",
        out_shape=jax.ShapeDtypeStruct((1, ROWS), F32),
        in_specs=[vmem] * 3,
        out_specs=vmem,
        scratch_shapes=[
            pltpu.VMEM((ROWS, DIM), BF16),
            pltpu.VMEM((NO * NS, ROWS), BF16),
            pltpu.VMEM((1, ROWS), jnp.int32),
            pltpu.VMEM((NO * BLOCK, QUART), BF16),
            pltpu.VMEM((NO * BLOCK, QUART), BF16),
            pltpu.VMEM((SLOTS, DIM), BF16),
            pltpu.VMEM((NS, 1, 128), F32),
            pltpu.VMEM((NS, 1, 128), F32),
            pltpu.VMEM((NO, NS, 1, 128), F32),
            pltpu.VMEM((SLOTS, 128), F32),
            pltpu.VMEM((SLOTS, 128), F32),
            pltpu.VMEM((1, SLOTS), F32),
            pltpu.VMEM((NS, 1, 128), F32),
            pltpu.VMEM((NS, 1, 128), F32),
            pltpu.VMEM((NO, NS, 1, 128), F32),
            dma((NO,)), dma((NO,)),
            dma, dma, dma, dma, dma, dma, dma, dma,
            pltpu.SemaphoreType.REGULAR,
        ],
        compiler_params=pltpu.CompilerParams(
            collective_id=0, has_side_effects=True, vmem_limit_bytes=48 << 20
        ),
        cost_estimate=pl.CostEstimate(
            flops=8 << 30, bytes_accessed=4 << 20, transcendentals=ROWS
        ),
    )(embeddings, cluster_id.reshape(1, ROWS), doc_order.reshape(1, ROWS))
    return out.reshape(ROWS)


def solution(mesh):
    in_specs = (P(("owner", "split"), None), P(("owner", "split")), P(("owner", "split")))
    out_specs = P(("owner", "split"))
    return jax.shard_map(local, mesh=mesh, in_specs=in_specs, out_specs=out_specs, check_vma=False)
```

time: 301 us -> 78.3 us (0.26)
  waiting for transfers between devices: 97.5 us -> 0 us
  blocking collectives: 93.2 us -> 0 us
  Pallas kernels: 0 us -> 75 us
  local copies, waits for them, and re-layouts: 64 us -> 3.17 us
  other arithmetic: 14.4 us -> 0 us
  between operations: 13.7 us -> 0.01 us
  starting transfers between devices: 13.2 us -> 0 us
  matrix products: 4.29 us -> 0 us
    all_gather x1 -> x0, waiting for transfers between devices: 87.2 us -> none  [local(): lax.all_gather(first_unit[None], 'split', axis=0, tiled=True)]
    pallas_call x0 -> x1, Pallas kernels: none -> 75 us  [local(): pl.pallas_call(kernel, name='dedup', out_shape=jax.ShapeDtypeStruct((1, R...]
    all_to_all x2 -> x0, blocking collectives: 47.6 us -> none  [the longest x1 34.9 us: local(): lax.all_to_all(packed[0], 'owner', split_axis=0, concat_axis=0, tiled=True)]
    all_gather x2 -> x0, blocking collectives: 45.6 us -> none  [the longest x1 26.8 us: local(): lax.all_gather(first_cluster[None], 'split', axis=0, tiled=True)]
    gather x6 -> x0, local copies, waits for them, and re-layouts: 27.1 us -> none  [the longest x1 5.36 us: local(): query_unit[sorting]]
    dynamic_slice x5 -> x0, local copies, waits for them, and re-layouts: 13.9 us -> none  [the longest x2 10 us: local(): lax.dynamic_index_in_dim(wide_unit, position, axis=2, keepdims=False)]
    all_to_all x3 -> x0, starting transfers between devices: 13.2 us -> none  [the longest x1 5.99 us: local(): lax.all_to_all(lax.all_to_all(highest.reshape(owner_count, split_count, c...]
    all_to_all x3 -> x0, waiting for transfers between devices: 10.3 us -> none  [the longest x1 7.38 us: local(): lax.all_to_all(lax.all_to_all(highest.reshape(owner_count, split_count, c...]
  transfers between devices with their start and end apart: 4 -> 0, of which waited for: 3 -> 0; matrix products, arithmetic and copies ran while one was open for 13% -> 0% of each run, Pallas kernels for 0% -> 0%
where the time goes in v1:
time: 78.3 us; the launch traced here: 78.1 us
  Pallas kernels  75 us (96%)
  local copies, waits for them, and re-layouts  3.17 us (4%)
    pallas_call x1, Pallas kernels, local(): pl.pallas_call(kernel, name='dedup', out_shape=jax.ShapeDtypeStruct((1, R...  75 us
    unnamed x7, local copies, waits for them, and re-layouts  3.17 us

profile of v1, /device:TPU:1, one launch (start us, length us, event | category | flops | bytes accessed | tf_op | source)
XLA Modules:
  0.0 78.1 jit_solution(11022690729062233718)
XLA Ops:
  0.0 0.0 copy-start.1
  0.0 0.7 copy-done.1
  0.7 0.0 copy-start
  0.7 1.2 %copy-done = bf16[512,1024]{1,0:T(8,128)(2,1)S(1)} copy-done((bf16[512,1024]{1,0:T(8,128)(2,1)S(1)}, bf16[512,1024]{1,0:T(8,128)(2,1)}, u32[]{:S(2)}) %copy-start) | copy-done | bytes 1048600
  1.9 0.0 copy-start.2
  1.9 0.7 copy-done.2
  2.6 75.0 %dedup.1 = f32[1,512]{1,0:T(1,128)S(1)} custom-call(bf16[512,1024]{1,0:T(8,128)(2,1)S(1)} %copy-done, s32[1,512]{1,0:T(1,128)S(1)} %bitcast.4, s32[1,512]{1,0:T(1,128)S(1)} %bitcast.5), custom_call_target="tpu_custom_call" | custom-call | flops 8589934592 | bytes 4194304 | tf_op jit(solution)/shard_map/dedup/pallas_call | solution.py:222
  77.6 0.6 copy.5
Async XLA Ops:
  0.0 0.7 copy-start.1
  0.7 1.2 %copy-start = (bf16[512,1024]{1,0:T(8,128)(2,1)S(1)}, bf16[512,1024]{1,0:T(8,128)(2,1)}, u32[]{:S(2)}) copy-start(bf16[512,1024]{1,0:T(8,128)(2,1)} %emb_ref.1) | copy-start | bytes 3145732
  1.9 0.7 copy-start.2

commit v2 on v1

v2 whole, which is shorter than its diff:
```python
import jax
import jax.numpy as jnp
from jax import lax
from jax.experimental import pallas as pl
from jax.experimental.pallas import tpu as pltpu
from jax.sharding import PartitionSpec as P

MESH = pl.DeviceIdType.MESH
F32 = jnp.float32
BF16 = jnp.bfloat16

NY, NX, NZ, NC = 4, 4, 8, 2
NO, NS = NY * NX, NZ * NC
CAP = 4
ROWS = 512
DIM = 1024
QUART = DIM // 4
SLOTS = NO * NS * CAP
UNIT = NS * CAP
SLAB = 16
BLOCK = NS * SLAB
CHIPS = NO * NZ


def distance(k):
    dy, dx = divmod(k, NX)
    return min(dy, NY - dy) + min(dx, NX - dx)


STEPS = [0] + sorted(range(1, NO), key=lambda k: -distance(k))
SPLITS = sorted(range(NS), key=lambda k: -min(k % NZ, NZ - k % NZ))


def iota(shape, dim):
    return lax.broadcasted_iota(jnp.int32, shape, dim)


def dot(a, b, contract):
    return lax.dot_general(a, b, ((contract[:1], contract[1:]), ((), ())), preferred_element_type=F32)


def ones_where(mask):
    return mask.astype(F32).astype(BF16)


def kernel(
    emb_hbm, clu_hbm, ord_hbm, out_ref,
    emb, clu_v, ord_v, onehot, slot, send, recv, keys, meta_out, meta_mid, meta_in, meta_col,
    best_col, best_row, swap_out, swap_in, ans_out, ans_in,
    in_sem, send_sem, recv_sem, ma_s, ma_r, mb_s, mb_r, sw_s, sw_r, an_s, an_r, ready,
):
    me_o = lax.axis_index("owner")
    me_s = lax.axis_index("split")
    y, x = me_o // NX, lax.rem(me_o, NX)
    z, c = me_s // NC, lax.rem(me_s, NC)

    def owner_at(k, sign=1):
        dy, dx = k // NX, k % NX
        if sign < 0:
            dy, dx = NY - dy, NX - dx
        return lax.rem(y + dy, NY) * NX + lax.rem(x + dx, NX)

    def split_at(k, sign=1):
        dc, dz = k // NZ, k % NZ
        if sign < 0:
            dz = NZ - dz
        return lax.rem(z + dz, NZ) * NC + lax.rem(c + dc, NC)

    def remote(src, dst, ssem, rsem, device):
        return pltpu.make_async_remote_copy(
            src_ref=src, dst_ref=dst, send_sem=ssem, recv_sem=rsem,
            device_id=device, device_id_type=MESH,
        )

    clu_in = pltpu.make_async_copy(clu_hbm, clu_v, in_sem.at[0])
    emb_in = pltpu.make_async_copy(emb_hbm, emb, in_sem.at[1])
    ord_in = pltpu.make_async_copy(ord_hbm, ord_v, in_sem.at[2])
    clu_in.start()
    emb_in.start()
    ord_in.start()

    barrier = pltpu.get_barrier_semaphore()
    for k in SPLITS:
        if k:
            pl.semaphore_signal(barrier, inc=1, device_id=(me_o, split_at(k)), device_id_type=MESH)
    for k in STEPS[1:]:
        pl.semaphore_signal(barrier, inc=1, device_id=(owner_at(k), me_s), device_id_type=MESH)

    before = ones_where(iota((ROWS, ROWS), 0) < iota((ROWS, ROWS), 1))
    row, col = iota((BLOCK, BLOCK), 0), iota((BLOCK, BLOCK), 1)
    weave = ones_where(col == ((row >> 2) & 3) * UNIT + (row & 3) * NS + (row >> 4))
    unweave = ones_where(row == ((col >> 2) & 3) * UNIT + (col & 3) * NS + (col >> 4))

    clu_in.wait()
    clu = clu_v[...]
    to_o = clu & (NO - 1)
    to_s = (clu >> 4) & (NS - 1)
    rel_y = ((to_o >> 2) - y) & (NY - 1)
    rel_x = ((to_o & (NX - 1)) - x) & (NX - 1)
    rel_z = ((to_s >> 1) - z) & (NZ - 1)
    rel_c = ((to_s & 1) - c) & 1
    k_o = rel_y * NX + rel_x
    k_s = rel_c * NZ + rel_z
    hot = (k_o * NS + k_s == iota((NO * NS, ROWS), 0)).astype(F32)
    count = dot(hot.astype(BF16), before, (1, 0))
    rank = jnp.sum(hot * count, axis=0, keepdims=True).astype(jnp.int32)
    slot[...] = k_o * UNIT + rank * NS + k_s

    def fill(b):
        choose = ones_where(slot[...] == b * UNIT + iota((UNIT, ROWS), 0))
        rows = dot(choose, emb[...], (1, 0))
        scale = lax.rsqrt(jnp.sum(rows * rows, axis=1, keepdims=True) + 1e-06)
        rows = (rows * scale).astype(BF16)
        quarters = jnp.concatenate([rows[:, q * QUART : (q + 1) * QUART] for q in range(4)], axis=0)
        send[b * BLOCK : (b + 1) * BLOCK] = dot(weave, quarters, (1, 0)).astype(BF16)

    def ship(b):
        for k in SPLITS:
            part = pl.ds(b * BLOCK + k * SLAB, SLAB)
            if b == 0 and k == 0:
                recv[part] = send[part]
                continue
            remote(
                send.at[part], recv.at[part], send_sem.at[b], recv_sem.at[b],
                (owner_at(b), split_at(k)),
            ).start()

    emb_in.wait()
    fill(0)
    pl.semaphore_wait(barrier, NS - 1 + NO - 1)
    for k in STEPS[1:]:
        pl.semaphore_signal(ready.at[k], inc=1, device_id=(owner_at(k, -1), me_s), device_id_type=MESH)
    ship(0)

    onehot[...] = ones_where(k_o * NZ + rel_z == iota((CHIPS, ROWS), 0))
    ord_in.wait()
    orders = ord_v[...]
    line = iota((8, ROWS), 0)
    code = clu + 1
    parts = jnp.where(
        line == 0, orders >> 12,
        jnp.where(line == 1, (orders >> 6) & 63,
                  jnp.where(line == 2, orders & 63,
                            jnp.where(line == 3, code >> 6,
                                      jnp.where(line == 4, code & 63, 0)))),
    ).astype(F32).astype(BF16)
    by_split = k_s * UNIT + k_o * CAP + rank
    pick = ones_where(by_split == iota((SLOTS, ROWS), 0))
    got = dot(parts, pick, (1, 1))
    slot_order = got[0:1] * 4096.0 + got[1:2] * 64.0 + got[2:3]
    slot_cluster = got[3:4] * 64.0 + got[4:5] - 1.0
    low = iota((1, 128), 1) < 64
    for p in range(NS // 2):
        a = slot_order[:, p * 128 : (p + 1) * 128]
        b = slot_cluster[:, p * 128 : (p + 1) * 128]
        meta_out[2 * p] = jnp.where(low, a, pltpu.roll(b, 64, 1))
        meta_out[2 * p + 1] = jnp.where(low, pltpu.roll(a, 64, 1), b)
    for k in SPLITS:
        if k:
            remote(meta_out.at[k], meta_mid.at[k], ma_s, ma_r, (me_o, split_at(k))).start()
    meta_mid[0] = meta_out[0]

    for b in STEPS[1:]:
        fill(b)
        pl.semaphore_wait(ready.at[b], 1)
        ship(b)

    some = remote(meta_out.at[pl.ds(1, NS - 1)], meta_mid.at[pl.ds(1, NS - 1)], ma_s, ma_r, (me_o, split_at(1)))
    some.wait_recv()
    for k in STEPS[1:]:
        remote(meta_mid, meta_in.at[k], mb_s, mb_r, (owner_at(k), me_s)).start()
    meta_in[0] = meta_mid[...]
    some.wait_send()
    many = remote(meta_in.at[pl.ds(1, NO - 1)], meta_in.at[pl.ds(1, NO - 1)], mb_s, mb_r, (owner_at(1), me_s))
    many.wait_recv()
    for i, b in enumerate(STEPS):
        lines = meta_in[b].reshape(NS, 128)
        for r in range(CAP):
            at = i * UNIT + r * NS
            lane = b * CAP + r
            meta_col[at : at + NS] = pltpu.roll(lines, 128 - lane, 1) if lane else lines
    many.wait_send()
    turned = meta_col[...].T
    row_order, row_cluster = turned[0:1], turned[64:65]

    best_row[...] = jnp.full((1, SLOTS), -1.0, F32)
    step = 2
    for g in range(0, NO, step):
        for i in range(g, g + step):
            b = STEPS[i]
            first = SLAB if b == 0 else 0
            span = pl.ds(b * BLOCK + first, BLOCK - first)
            remote(
                send.at[span], recv.at[span], send_sem.at[b], recv_sem.at[b], (me_o, split_at(1))
            ).wait_recv()
            woven = dot(unweave, recv[b * BLOCK : (b + 1) * BLOCK], (1, 0)).astype(BF16)
            for q in range(4):
                keys[i * UNIT : (i + 1) * UNIT, q * QUART : (q + 1) * QUART] = woven[
                    q * UNIT : (q + 1) * UNIT
                ]
        lo, hi = g * UNIT, (g + step) * UNIT
        score = dot(keys[lo:hi], keys[0:hi], (1, 1))
        new_order, new_cluster = meta_col[lo:hi, 0:1], meta_col[lo:hi, 64:65]
        old_order, old_cluster = row_order[:, :hi], row_cluster[:, :hi]
        score = jnp.where(new_cluster == old_cluster, score, -1.0)
        best = jnp.max(jnp.where(old_order < new_order, score, -1.0), axis=1, keepdims=True)
        best_col[lo:hi] = jnp.broadcast_to(best, (hi - lo, 128))
        best = jnp.max(jnp.where(new_order < old_order, score, -1.0), axis=0, keepdims=True)
        best_row[:, :hi] = jnp.maximum(best_row[:, :hi], best)

    final = jnp.maximum(best_col[...], jnp.broadcast_to(best_row[...], (128, SLOTS)).T)
    lanes = iota((NZ, 128), 1)
    for i, b in enumerate(STEPS):
        stay = jnp.zeros((NZ, 128), F32)
        leave = jnp.zeros((NZ, 128), F32)
        for r in range(CAP):
            at = i * UNIT + r * NS
            stay = jnp.where(lanes == r, final[at : at + NZ], stay)
            leave = jnp.where(lanes == CAP + r, final[at + NZ : at + NS], leave)
        swap_out[b * NZ : (b + 1) * NZ] = leave
        best_col[b * NZ : (b + 1) * NZ] = stay
    swap = remote(swap_out, swap_in, sw_s, sw_r, (me_o, split_at(NZ)))
    swap.start()
    swap.wait_recv()
    both = best_col[0:CHIPS] + swap_in[...]
    ans_out[...] = both.reshape(CHIPS, 1, 128)
    ways = sorted(range(1, CHIPS), key=lambda k: -distance(k // NZ) - min(k % NZ, NZ - k % NZ))
    for k in ways:
        remote(
            ans_out.at[k], ans_in.at[k], an_s, an_r, (owner_at(k // NZ, -1), split_at(k % NZ, -1))
        ).start()
    ans_in[0] = ans_out[0]
    swap.wait_send()
    for b in range(NO):
        first = SLAB if b == 0 else 0
        span = pl.ds(b * BLOCK + first, BLOCK - first)
        remote(
            send.at[span], recv.at[span], send_sem.at[b], recv_sem.at[b], (me_o, split_at(1))
        ).wait_send()
    most = pl.ds(1, CHIPS - 1)
    answers = remote(ans_out.at[most], ans_in.at[most], an_s, an_r, (me_o, split_at(1)))
    answers.wait_recv()

    table = ans_in[...].reshape(CHIPS, 128).T[0:8]
    high = table.astype(BF16)
    rest = table - high.astype(F32)
    mid = rest.astype(BF16)
    tiny = (rest - mid.astype(F32)).astype(BF16)
    mine = dot(high, onehot[...], (1, 0)) + dot(mid, onehot[...], (1, 0)) + dot(tiny, onehot[...], (1, 0))
    out_ref[...] = jnp.sum(jnp.where(line == rel_c * CAP + rank, mine, 0.0), axis=0, keepdims=True)
    answers.wait_send()


def local(embeddings, cluster_id, doc_order):
    hbm = pl.BlockSpec(memory_space=pltpu.HBM)
    dma = pltpu.SemaphoreType.DMA
    out = pl.pallas_call(
        kernel,
        name="dedup",
        out_shape=jax.ShapeDtypeStruct((1, ROWS), F32),
        in_specs=[hbm] * 3,
        out_specs=pl.BlockSpec(memory_space=pltpu.VMEM),
        scratch_shapes=[
            pltpu.VMEM((ROWS, DIM), BF16),
            pltpu.VMEM((1, ROWS), jnp.int32),
            pltpu.VMEM((1, ROWS), jnp.int32),
            pltpu.VMEM((CHIPS, ROWS), BF16),
            pltpu.VMEM((1, ROWS), jnp.int32),
            pltpu.VMEM((NO * BLOCK, QUART), BF16),
            pltpu.VMEM((NO * BLOCK, QUART), BF16),
            pltpu.VMEM((SLOTS, DIM), BF16),
            pltpu.VMEM((NS, 1, 128), F32),
            pltpu.VMEM((NS, 1, 128), F32),
            pltpu.VMEM((NO, NS, 1, 128), F32),
            pltpu.VMEM((SLOTS, 128), F32),
            pltpu.VMEM((SLOTS, 128), F32),
            pltpu.VMEM((1, SLOTS), F32),
            pltpu.VMEM((CHIPS, 128), F32),
            pltpu.VMEM((CHIPS, 128), F32),
            pltpu.VMEM((CHIPS, 1, 128), F32),
            pltpu.VMEM((CHIPS, 1, 128), F32),
            dma((3,)), dma((NO,)), dma((NO,)),
            dma, dma, dma, dma, dma, dma, dma, dma,
            pltpu.SemaphoreType.REGULAR((NO,)),
        ],
        compiler_params=pltpu.CompilerParams(
            collective_id=0, has_side_effects=True, vmem_limit_bytes=56 << 20
        ),
        cost_estimate=pl.CostEstimate(
            flops=8 << 30, bytes_accessed=4 << 20, transcendentals=SLOTS
        ),
    )(embeddings, cluster_id.reshape(1, ROWS), doc_order.reshape(1, ROWS))
    return out.reshape(ROWS)


def solution(mesh):
    in_specs = (P(("owner", "split"), None), P(("owner", "split")), P(("owner", "split")))
    out_specs = P(("owner", "split"))
    return jax.shard_map(local, mesh=mesh, in_specs=in_specs, out_specs=out_specs, check_vma=False)
```

time: 78.3 us -> 70.6 us (0.902)
  Pallas kernels: 75 us -> 69.2 us
  local copies, waits for them, and re-layouts: 3.17 us -> 1.26 us
    pallas_call x1, Pallas kernels: 75 us -> 69.2 us  [local(): pl.pallas_call(kernel, name='dedup', out_shape=jax.ShapeDtypeStruct((1, R...]
    unnamed x7 -> x1, local copies, waits for them, and re-layouts: 3.17 us -> 1.26 us
where the time goes in v2:
time: 70.6 us; the launch traced here: 70.5 us
  Pallas kernels  69.2 us (98%)
  local copies, waits for them, and re-layouts  1.26 us (2%)
    pallas_call x1, Pallas kernels, local(): pl.pallas_call(kernel, name='dedup', out_shape=jax.ShapeDtypeStruct((1, R...  69.2 us

profile of v2, /device:TPU:1, one launch (start us, length us, event | category | flops | bytes accessed | tf_op | source)
XLA Modules:
  0.0 70.5 jit_solution(4196442797374857780)
XLA Ops:
  0.0 69.2 %dedup.1 = f32[1,512]{1,0:T(1,128)} custom-call(bf16[512,1024]{1,0:T(8,128)(2,1)} %emb_hbm.1, s32[1,512]{1,0:T(1,128)} %bitcast.4, s32[1,512]{1,0:T(1,128)} %bitcast.5), custom_call_target="tpu_custom_call" | custom-call | flops 8589934592 | bytes 4194304 | tf_op jit(solution)/shard_map/dedup/pallas_call | solution.py:257
  69.2 1.3 %copy.5 = f32[512]{0:T(512)} copy(f32[512]{0:T(512)} %bitcast.3) | data formatting | bytes 4096

commit v3 on v2

--- a/solution.py
+++ b/solution.py
@@ -21,6 +21,20 @@
 BLOCK = NS * SLAB
 CHIPS = NO * NZ
 
+NEAR = 2
+PAIR = NS * NEAR
+LEAF = 16
+EIGHTH = DIM // 8
+POOL = 32
+POOLED = NZ * POOL
+TAIL = NZ * (CAP - NEAR)
+BLOCKS = NO * NC
+FIRST = 8
+EARLY = 12
+POOL_AT = EARLY * PAIR
+FLAG = 2.0**18
+REDO = 4.0
+
 
 def distance(k):
     dy, dx = divmod(k, NX)
@@ -43,7 +57,7 @@
     return mask.astype(F32).astype(BF16)
 
 
-def kernel(
+def full_kernel(
     emb_hbm, clu_hbm, ord_hbm, out_ref,
     emb, clu_v, ord_v, onehot, slot, send, recv, keys, meta_out, meta_mid, meta_in, meta_col,
     best_col, best_row, swap_out, swap_in, ans_out, ans_in,
@@ -251,46 +265,396 @@
     answers.wait_send()
 
 
-def local(embeddings, cluster_id, doc_order):
+def pooled_kernel(
+    emb_hbm, clu_hbm, ord_hbm, out_ref,
+    emb, clu_v, ord_v, onehot, slot, send, recv, keys, meta_out, meta_mid, meta_in, meta_col,
+    best_col, best_row, swap_out, swap_in, ans_out, ans_in, pool_out, pool_in, id_out, id_in, tail_out,
+    col_order, col_cluster,
+    in_sem, send_sem, recv_sem, ma_s, ma_r, mb_s, mb_r, sw_s, sw_r, an_s, an_r,
+    po_s, po_r, id_s, id_r, ta_s, ta_r, ready,
+):
+    me_o = lax.axis_index("owner")
+    me_s = lax.axis_index("split")
+    y, x = me_o // NX, lax.rem(me_o, NX)
+    z, c = me_s // NC, lax.rem(me_s, NC)
+
+    def owner_at(k, sign=1):
+        dy, dx = k // NX, k % NX
+        if sign < 0:
+            dy, dx = NY - dy, NX - dx
+        return lax.rem(y + dy, NY) * NX + lax.rem(x + dx, NX)
+
+    def split_at(k, sign=1):
+        dc, dz = k // NZ, k % NZ
+        if sign < 0:
+            dz = NZ - dz
+        return lax.rem(z + dz, NZ) * NC + lax.rem(c + dc, NC)
+
+    def remote(src, dst, ssem, rsem, device):
+        return pltpu.make_async_remote_copy(
+            src_ref=src, dst_ref=dst, send_sem=ssem, recv_sem=rsem,
+            device_id=device, device_id_type=MESH,
+        )
+
+    clu_in = pltpu.make_async_copy(clu_hbm, clu_v, in_sem.at[0])
+    emb_in = pltpu.make_async_copy(emb_hbm, emb, in_sem.at[1])
+    ord_in = pltpu.make_async_copy(ord_hbm, ord_v, in_sem.at[2])
+    clu_in.start()
+    emb_in.start()
+    ord_in.start()
+
+    barrier = pltpu.get_barrier_semaphore()
+    for k in SPLITS:
+        if k:
+            pl.semaphore_signal(barrier, inc=1, device_id=(me_o, split_at(k)), device_id_type=MESH)
+    for k in STEPS[1:]:
+        pl.semaphore_signal(barrier, inc=1, device_id=(owner_at(k), me_s), device_id_type=MESH)
+
+    before = ones_where(iota((ROWS, ROWS), 0) < iota((ROWS, ROWS), 1))
+    row, col = iota((BLOCK, BLOCK), 0), iota((BLOCK, BLOCK), 1)
+    weave = ones_where(col == ((row >> 1) & 7) * PAIR + (row & 1) * NS + (row >> 4))
+    unweave = ones_where(row == ((col >> 1) & 7) * PAIR + (col & 1) * NS + (col >> 4))
+
+    clu_in.wait()
+    clu = clu_v[...]
+    to_o = clu & (NO - 1)
+    to_s = (clu >> 4) & (NS - 1)
+    rel_y = ((to_o >> 2) - y) & (NY - 1)
+    rel_x = ((to_o & (NX - 1)) - x) & (NX - 1)
+    rel_z = ((to_s >> 1) - z) & (NZ - 1)
+    rel_c = ((to_s & 1) - c) & 1
+    k_o = rel_y * NX + rel_x
+    k_s = rel_c * NZ + rel_z
+    hot = (k_o * NS + k_s == iota((NO * NS, ROWS), 0)).astype(F32)
+    count = dot(hot.astype(BF16), before, (1, 0))
+    rank = jnp.sum(hot * count, axis=0, keepdims=True).astype(jnp.int32)
+    near = rank < NEAR
+    slot[...] = jnp.where(near, k_o * PAIR + rank * NS + k_s, -1)
+
+    hot = jnp.where((rel_z == iota((NZ, ROWS), 0)) & (rank >= NEAR), 1.0, 0.0)
+    count = dot(hot.astype(BF16), before, (1, 0))
+    place = jnp.sum(hot * count, axis=0, keepdims=True).astype(jnp.int32)
+    over = jnp.max(jnp.sum(hot, axis=1, keepdims=True), axis=0, keepdims=True) > POOL
+    pool = jnp.where((rank >= NEAR) & (place < POOL), rel_z * POOL + place, -1)
+    code = (k_o * NC + rel_c) * TAIL + (rank - NEAR) * NZ + rel_z + 1
+    line = iota((8, ROWS), 0)
+    parts = jnp.where(line == 0, code >> 6, jnp.where(line == 1, code & 63, 0)).astype(F32).astype(BF16)
+    choose = ones_where(pool == iota((POOLED, ROWS), 0))
+    got = dot(parts, choose, (1, 1))
+    ids = got[0:1] * 64.0 + got[1:2] - 1.0
+    for k in range(NZ):
+        half = k * POOL // 128
+        id_out[k] = ids[:, half * 128 : (half + 1) * 128]
+
+    def normal(rows):
+        scale = lax.rsqrt(jnp.sum(rows * rows, axis=1, keepdims=True) + 1e-06)
+        return (rows * scale).astype(BF16)
+
+    emb_in.wait()
+    pool_out[...] = normal(dot(choose, emb[...], (1, 0)))
+    pl.semaphore_wait(barrier, NS - 1 + NO - 1)
+    for k in SPLITS:
+        if 0 < k < NZ:
+            part = pl.ds(k * POOL, POOL)
+            remote(pool_out.at[part], pool_in.at[part], po_s, po_r, (me_o, split_at(k))).start()
+            remote(id_out.at[k], id_in.at[k], id_s, id_r, (me_o, split_at(k))).start()
+    for k in STEPS[1:]:
+        pl.semaphore_signal(ready.at[k], inc=1, device_id=(owner_at(k, -1), me_s), device_id_type=MESH)
+    pool_in[0:POOL] = pool_out[0:POOL]
+    id_in[0] = id_out[0]
+
+    def fill(first):
+        steps = STEPS[first : first + 4]
+        at = iota((PAIR, ROWS), 0)
+        choose = jnp.concatenate([ones_where(slot[...] == b * PAIR + at) for b in steps], axis=0)
+        rows = normal(dot(choose, emb[...], (1, 0)))
+        for n, b in enumerate(steps):
+            mine = rows[n * PAIR : (n + 1) * PAIR]
+            parts = jnp.concatenate([mine[:, q * EIGHTH : (q + 1) * EIGHTH] for q in range(8)], axis=0)
+            send[b * BLOCK : (b + 1) * BLOCK] = dot(weave, parts, (1, 0)).astype(BF16)
+
+    def ship(b, k):
+        part = pl.ds(b * BLOCK + k * LEAF, LEAF)
+        if b == 0 and k == 0:
+            recv[part] = send[part]
+            return
+        remote(
+            send.at[part], recv.at[part], send_sem.at[b], recv_sem.at[b],
+            (owner_at(b), split_at(k)),
+        ).start()
+
+    def ship_tail(k):
+        part = pl.ds(k * TAIL, TAIL)
+        goal = pl.ds(POOL_AT + k * TAIL, TAIL)
+        if k == 0:
+            keys[goal] = tail_out[part]
+            return
+        remote(
+            tail_out.at[part], keys.at[goal], ta_s, ta_r, (owner_at(k // NC), split_at(k % NC * NZ))
+        ).start()
+
+    fill(0)
+    for b in STEPS[0:4]:
+        if b:
+            pl.semaphore_wait(ready.at[b], 1)
+        for k in SPLITS:
+            ship(b, k)
+
+    onehot[...] = ones_where(k_o * NZ + rel_z == iota((CHIPS, ROWS), 0))
+    ord_in.wait()
+    orders = ord_v[...]
+    code = clu + 1
+    parts = jnp.where(
+        line == 0, orders >> 12,
+        jnp.where(line == 1, (orders >> 6) & 63,
+                  jnp.where(line == 2, orders & 63,
+                            jnp.where(line == 3, code >> 6,
+                                      jnp.where(line == 4, code & 63, 0)))),
+    ).astype(F32).astype(BF16)
+    by_split = k_s * UNIT + k_o * CAP + rank
+    pick = ones_where(by_split == iota((SLOTS, ROWS), 0))
+    got = dot(parts, pick, (1, 1))
+    slot_order = got[0:1] * 4096.0 + got[1:2] * 64.0 + got[2:3] + jnp.where(over, FLAG, 0.0)
+    slot_cluster = got[3:4] * 64.0 + got[4:5] - 1.0
+    low = iota((1, 128), 1) < 64
+    for p in range(NS // 2):
+        a = slot_order[:, p * 128 : (p + 1) * 128]
+        b = slot_cluster[:, p * 128 : (p + 1) * 128]
+        meta_out[2 * p] = jnp.where(low, a, pltpu.roll(b, 64, 1))
+        meta_out[2 * p + 1] = jnp.where(low, pltpu.roll(a, 64, 1), b)
+    for k in SPLITS:
+        if k:
+            remote(meta_out.at[k], meta_mid.at[k], ma_s, ma_r, (me_o, split_at(k))).start()
+    meta_mid[0] = meta_out[0]
+
+    fill(4)
+    fill(8)
+    fill(12)
+    for b in STEPS[4:]:
+        pl.semaphore_wait(ready.at[b], 1)
+    for b in STEPS[4:FIRST]:
+        for k in SPLITS:
+            ship(b, k)
+
+    some = remote(meta_out.at[pl.ds(1, NS - 1)], meta_mid.at[pl.ds(1, NS - 1)], ma_s, ma_r, (me_o, split_at(1)))
+    some.wait_recv()
+    for k in STEPS[1:]:
+        remote(meta_mid, meta_in.at[k], mb_s, mb_r, (owner_at(k), me_s)).start()
+    meta_in[0] = meta_mid[...]
+    some.wait_send()
+    wide, thin = pl.ds(POOL, POOLED - POOL), pl.ds(1, NZ - 1)
+    pools = remote(pool_out.at[wide], pool_in.at[wide], po_s, po_r, (me_o, split_at(1)))
+    names = remote(id_out.at[thin], id_in.at[thin], id_s, id_r, (me_o, split_at(1)))
+    names.wait_recv()
+    part = iota((1, 128), 1) // POOL
+    ids = []
+    for half in range(POOLED // 128):
+        lane_ids = id_in[half * 4]
+        for k in range(1, 4):
+            lane_ids = jnp.where(part == k, id_in[half * 4 + k], lane_ids)
+        ids.append(lane_ids)
+    ids = jnp.concatenate(ids, axis=1).astype(jnp.int32)
+    choose = ones_where(ids == iota((BLOCKS * TAIL, POOLED), 0))
+    pools.wait_recv()
+    tail_out[...] = dot(choose, pool_in[...], (1, 0)).astype(BF16)
+    rest = [(b, k) for b in STEPS[FIRST:] for k in SPLITS]
+    blocks = [b * NC + kc for b in STEPS for kc in range(NC)]
+    for n, k in enumerate(blocks):
+        ship_tail(k)
+        for pair in rest[n * len(rest) // BLOCKS : (n + 1) * len(rest) // BLOCKS]:
+            ship(*pair)
+
+    many = remote(meta_in.at[pl.ds(1, NO - 1)], meta_in.at[pl.ds(1, NO - 1)], mb_s, mb_r, (owner_at(1), me_s))
+    many.wait_recv()
+    widest = jnp.full((NS, 128), -1.0, F32)
+    for i, b in enumerate(STEPS):
+        lines = meta_in[b].reshape(NS, 128)
+        widest = jnp.maximum(widest, lines)
+        for r in range(CAP):
+            lane = b * CAP + r
+            turned = pltpu.roll(lines, 128 - lane, 1) if lane else lines
+            if r < NEAR:
+                at = i * PAIR + r * NS + (BLOCKS * TAIL if i >= EARLY else 0)
+                meta_col[at : at + NS] = turned
+            else:
+                for kc in range(NC):
+                    at = POOL_AT + (b * NC + kc) * TAIL + (r - NEAR) * NZ
+                    meta_col[at : at + NZ] = turned[kc * NZ : (kc + 1) * NZ]
+    many.wait_send()
+    widest = jnp.max(jnp.max(widest, axis=1, keepdims=True), axis=0, keepdims=True)
+    turned = meta_col[...].T
+    row_order, row_cluster = turned[0:1], turned[64:65]
+    col_order[...] = jnp.broadcast_to(meta_col[:, 0:1], (SLOTS, 128))
+    col_cluster[...] = jnp.broadcast_to(meta_col[:, 64:65], (SLOTS, 128))
+
+
+    def take(i):
+        b = STEPS[i]
+        first = LEAF if b == 0 else 0
+        span = pl.ds(b * BLOCK + first, BLOCK - first)
+        remote(
+            send.at[span], recv.at[span], send_sem.at[b], recv_sem.at[b], (me_o, split_at(1))
+        ).wait_recv()
+        woven = dot(unweave, recv[b * BLOCK : (b + 1) * BLOCK], (1, 0)).astype(BF16)
+        at = i * PAIR + (BLOCKS * TAIL if i >= EARLY else 0)
+        for q in range(8):
+            keys[at : at + PAIR, q * EIGHTH : (q + 1) * EIGHTH] = woven[q * PAIR : (q + 1) * PAIR]
+
+    def grade(lo, hi):
+        scores = dot(keys[0:hi], keys[lo:hi], (1, 1))
+        for at in range(lo, hi, 128):
+            span = slice(at, at + 128)
+            new_order, new_cluster = row_order[:, span], row_cluster[:, span]
+            score = jnp.where(col_cluster[0:hi] == new_cluster, scores[:, at - lo : at - lo + 128], -1.0)
+            earlier = col_order[0:hi] < new_order
+            best_row[:, span] = jnp.max(jnp.where(earlier, score, -1.0), axis=0, keepdims=True)
+            later = new_order < col_order[0:hi]
+            best_col[0:hi] = jnp.maximum(best_col[0:hi], jnp.where(later, score, -1.0))
+
+    best_col[...] = jnp.full((SLOTS, 128), -1.0, F32)
+    for i in range(8):
+        take(i)
+    grade(0, 8 * PAIR)
+    for i in range(8, EARLY):
+        take(i)
+    grade(8 * PAIR, POOL_AT)
+    span = pl.ds(POOL_AT + TAIL, (BLOCKS - 1) * TAIL)
+    tails = remote(
+        tail_out.at[pl.ds(TAIL, (BLOCKS - 1) * TAIL)], keys.at[span], ta_s, ta_r, (me_o, split_at(1))
+    )
+    tails.wait_recv()
+    grade(POOL_AT, POOL_AT + 256)
+    grade(POOL_AT + 256, POOL_AT + 512)
+    for i in range(EARLY, NO):
+        take(i)
+    grade(POOL_AT + 512, SLOTS)
+
+    final = jnp.max(best_col[...], axis=1, keepdims=True)
+    final = jnp.maximum(final, jnp.broadcast_to(best_row[...], (128, SLOTS)).T)
+    lanes = iota((NZ, 128), 1)
+    for i, b in enumerate(STEPS):
+        stay = jnp.zeros((NZ, 128), F32)
+        leave = jnp.zeros((NZ, 128), F32)
+        for r in range(CAP):
+            if r < NEAR:
+                at = i * PAIR + r * NS + (BLOCKS * TAIL if i >= EARLY else 0)
+                gap = NZ
+            else:
+                at = POOL_AT + b * NC * TAIL + (r - NEAR) * NZ
+                gap = TAIL
+            stay = jnp.where(lanes == r, final[at : at + NZ], stay)
+            leave = jnp.where(lanes == CAP + r, final[at + gap : at + gap + NZ], leave)
+        swap_out[b * NZ : (b + 1) * NZ] = leave
+        best_col[b * NZ : (b + 1) * NZ] = stay
+    swap = remote(swap_out, swap_in, sw_s, sw_r, (me_o, split_at(NZ)))
+    swap.start()
+    swap.wait_recv()
+    both = best_col[0:CHIPS] + swap_in[...]
+    ans_out[...] = both.reshape(CHIPS, 1, 128)
+    ways = sorted(range(1, CHIPS), key=lambda k: -distance(k // NZ) - min(k % NZ, NZ - k % NZ))
+    for k in ways:
+        remote(
+            ans_out.at[k], ans_in.at[k], an_s, an_r, (owner_at(k // NZ, -1), split_at(k % NZ, -1))
+        ).start()
+    ans_in[0] = ans_out[0]
+    swap.wait_send()
+    tails.wait_send()
+    pools.wait_send()
+    names.wait_send()
+    for b in range(NO):
+        first = LEAF if b == 0 else 0
+        span = pl.ds(b * BLOCK + first, BLOCK - first)
+        remote(
+            send.at[span], recv.at[span], send_sem.at[b], recv_sem.at[b], (me_o, split_at(1))
+        ).wait_send()
+    most = pl.ds(1, CHIPS - 1)
+    answers = remote(ans_out.at[most], ans_in.at[most], an_s, an_r, (me_o, split_at(1)))
+    answers.wait_recv()
+
+    table = ans_in[...].reshape(CHIPS, 128).T[0:8]
+    high = table.astype(BF16)
+    rest = table - high.astype(F32)
+    mid = rest.astype(BF16)
+    tiny = (rest - mid.astype(F32)).astype(BF16)
+    mine = dot(high, onehot[...], (1, 0)) + dot(mid, onehot[...], (1, 0)) + dot(tiny, onehot[...], (1, 0))
+    mine = jnp.sum(jnp.where(line == rel_c * CAP + rank, mine, 0.0), axis=0, keepdims=True)
+    out_ref[...] = jnp.where(widest >= FLAG, REDO, mine)
+    answers.wait_send()
+
+
+def common(rows, width):
+    return [
+        pltpu.VMEM((ROWS, DIM), BF16),
+        pltpu.VMEM((1, ROWS), jnp.int32),
+        pltpu.VMEM((1, ROWS), jnp.int32),
+        pltpu.VMEM((CHIPS, ROWS), BF16),
+        pltpu.VMEM((1, ROWS), jnp.int32),
+        pltpu.VMEM((rows, width), BF16),
+        pltpu.VMEM((rows, width), BF16),
+        pltpu.VMEM((SLOTS, DIM), BF16),
+        pltpu.VMEM((NS, 1, 128), F32),
+        pltpu.VMEM((NS, 1, 128), F32),
+        pltpu.VMEM((NO, NS, 1, 128), F32),
+        pltpu.VMEM((SLOTS, 128), F32),
+        pltpu.VMEM((SLOTS, 128), F32),
+        pltpu.VMEM((1, SLOTS), F32),
+        pltpu.VMEM((CHIPS, 128), F32),
+        pltpu.VMEM((CHIPS, 128), F32),
+        pltpu.VMEM((CHIPS, 1, 128), F32),
+        pltpu.VMEM((CHIPS, 1, 128), F32),
+    ]
+
+
+def call(kernel, name, number, outs, scratch, args):
     hbm = pl.BlockSpec(memory_space=pltpu.HBM)
-    dma = pltpu.SemaphoreType.DMA
-    out = pl.pallas_call(
+    vmem = pl.BlockSpec(memory_space=pltpu.VMEM)
+    return pl.pallas_call(
         kernel,
-        name="dedup",
-        out_shape=jax.ShapeDtypeStruct((1, ROWS), F32),
+        name=name,
+        out_shape=outs,
         in_specs=[hbm] * 3,
-        out_specs=pl.BlockSpec(memory_space=pltpu.VMEM),
-        scratch_shapes=[
-            pltpu.VMEM((ROWS, DIM), BF16),
-            pltpu.VMEM((1, ROWS), jnp.int32),
-            pltpu.VMEM((1, ROWS), jnp.int32),
-            pltpu.VMEM((CHIPS, ROWS), BF16),
-            pltpu.VMEM((1, ROWS), jnp.int32),
-            pltpu.VMEM((NO * BLOCK, QUART), BF16),
-            pltpu.VMEM((NO * BLOCK, QUART), BF16),
-            pltpu.VMEM((SLOTS, DIM), BF16),
-            pltpu.VMEM((NS, 1, 128), F32),
-            pltpu.VMEM((NS, 1, 128), F32),
-            pltpu.VMEM((NO, NS, 1, 128), F32),
-            pltpu.VMEM((SLOTS, 128), F32),
-            pltpu.VMEM((SLOTS, 128), F32),
-            pltpu.VMEM((1, SLOTS), F32),
-            pltpu.VMEM((CHIPS, 128), F32),
-            pltpu.VMEM((CHIPS, 128), F32),
-            pltpu.VMEM((CHIPS, 1, 128), F32),
-            pltpu.VMEM((CHIPS, 1, 128), F32),
-            dma((3,)), dma((NO,)), dma((NO,)),
-            dma, dma, dma, dma, dma, dma, dma, dma,
-            pltpu.SemaphoreType.REGULAR((NO,)),
-        ],
+        out_specs=[vmem] * len(outs),
+        scratch_shapes=scratch,
         compiler_params=pltpu.CompilerParams(
-            collective_id=0, has_side_effects=True, vmem_limit_bytes=56 << 20
+            collective_id=number, has_side_effects=True, vmem_limit_bytes=56 << 20
         ),
         cost_estimate=pl.CostEstimate(
             flops=8 << 30, bytes_accessed=4 << 20, transcendentals=SLOTS
         ),
-    )(embeddings, cluster_id.reshape(1, ROWS), doc_order.reshape(1, ROWS))
-    return out.reshape(ROWS)
+    )(*args)
+
+
+def local(embeddings, cluster_id, doc_order):
+    args = (embeddings, cluster_id.reshape(1, ROWS), doc_order.reshape(1, ROWS))
+    dma = pltpu.SemaphoreType.DMA
+    ready = pltpu.SemaphoreType.REGULAR((NO,))
+    result = jax.ShapeDtypeStruct((1, ROWS), F32)
+    pooled_scratch = common(NO * BLOCK, EIGHTH) + [
+        pltpu.VMEM((POOLED, DIM), BF16),
+        pltpu.VMEM((POOLED, DIM), BF16),
+        pltpu.VMEM((NZ, 1, 128), F32),
+        pltpu.VMEM((NZ, 1, 128), F32),
+        pltpu.VMEM((BLOCKS * TAIL, DIM), BF16),
+        pltpu.VMEM((SLOTS, 128), F32),
+        pltpu.VMEM((SLOTS, 128), F32),
+        dma((3,)), dma((NO,)), dma((NO,)),
+        *[dma] * 14,
+        ready,
+    ]
+    full_scratch = common(NO * BLOCK, QUART) + [
+        dma((3,)), dma((NO,)), dma((NO,)),
+        *[dma] * 8,
+        ready,
+    ]
+    best = call(pooled_kernel, "pooled", 0, [result], pooled_scratch, args)[0]
+
+    def again(args, best):
+        return call(full_kernel, "full", 1, [result], full_scratch, args)[0]
+
+    def keep(args, best):
+        return best
+
+    return lax.cond(best[0, 0] > REDO / 2, again, keep, args, best).reshape(ROWS)
 
 
 def solution(mesh):

time: 70.6 us -> 67.2 us (0.952)
  Pallas kernels: 69.2 us -> 64.4 us
    pallas_call x1, Pallas kernels: 69.2 us -> 64.4 us  [call(): pl.pallas_call(kernel, name=name, out_shape=outs, in_specs=[hbm] * 3, out...]
where the time goes in v3:
time: 67.2 us; the launch traced here: 67.1 us
  Pallas kernels  64.4 us (96%)
  local copies, waits for them, and re-layouts  1.79 us (3%)
  between operations  0.68 us (1%)
    pallas_call x1, Pallas kernels, call(): pl.pallas_call(kernel, name=name, out_shape=outs, in_specs=[hbm] * 3, out...  64.4 us

profile of v3, /device:TPU:1, one launch (start us, length us, event | category | flops | bytes accessed | tf_op | source)
XLA Modules:
  0.0 67.1 jit_solution(13188956908053015650)
XLA Ops:
  0.0 0.0 copy-start.2
  0.0 0.0 copy-start.1
  0.0 0.7 %copy-done.2 = s32[512]{0:T(512)S(1)} copy-done((s32[512]{0:T(512)S(1)}, s32[512]{0:T(512)}, u32[]{:S(2)}) %copy-start.2) | copy-done | bytes 2072
  0.7 0.0 copy-done.1
  0.7 0.0 copy-start
  0.7 64.4 %pooled.1 = f32[1,512]{1,0:T(1,128)S(1)} custom-call(bf16[512,1024]{1,0:T(8,128)(2,1)} %emb_hbm.1, s32[1,512]{1,0:T(1,128)S(1)} %bitcast.7, s32[1,512]{1,0:T(1,128)S(1)} %bitcast.9), custom_call_target="tpu_custom_call" | custom-call | flops 8589934592 | bytes 4194304 | tf_op jit(solution)/shard_map/pooled/pallas_call | solution.py:611
  65.1 0.5 slice.3
  66.3 0.0 copy-done
  66.3 0.2 conditional.1
  66.5 0.6 copy.10
Async XLA Ops:
  0.0 0.7 %copy-start.2 = (s32[512]{0:T(512)S(1)}, s32[512]{0:T(512)}, u32[]{:S(2)}) copy-start(s32[512]{0:T(512)} %param.7) | copy-start | bytes 6148
  0.0 0.7 %copy-start.1 = (s32[512]{0:T(512)S(1)}, s32[512]{0:T(512)}, u32[]{:S(2)}) copy-start(s32[512]{0:T(512)} %param.6) | copy-start | bytes 6148
  0.7 65.6 %copy-start = (bf16[512,1024]{1,0:T(8,128)(2,1)S(1)}, bf16[512,1024]{1,0:T(8,128)(2,1)}, u32[]{:S(2)}) copy-start(bf16[512,1024]{1,0:T(8,128)(2,1)} %emb_hbm.1) | copy-start | bytes 3145732

commit v4 on v3

--- a/solution.py
+++ b/solution.py
@@ -43,6 +43,14 @@
 
 STEPS = [0] + sorted(range(1, NO), key=lambda k: -distance(k))
 SPLITS = sorted(range(NS), key=lambda k: -min(k % NZ, NZ - k % NZ))
+
+
+def hops(k):
+    return distance(k // NZ) + min(k % NZ, NZ - k % NZ)
+
+
+WAYS = sorted(range(1, CHIPS), key=lambda k: -hops(k))
+FAR = [k for k in WAYS if hops(k) >= 6]
 
 
 def iota(shape, dim):
@@ -266,12 +274,12 @@
 
 
 def pooled_kernel(
-    emb_hbm, clu_hbm, ord_hbm, out_ref,
-    emb, clu_v, ord_v, onehot, slot, send, recv, keys, meta_out, meta_mid, meta_in, meta_col,
+    emb_hbm, clu_ref, ord_ref, out_ref,
+    emb, onehot, slot, send, recv, keys, meta_out, meta_mid, meta_in, meta_col,
     best_col, best_row, swap_out, swap_in, ans_out, ans_in, pool_out, pool_in, id_out, id_in, tail_out,
-    col_order, col_cluster,
+    col_order, col_cluster, far_out, far_in,
     in_sem, send_sem, recv_sem, ma_s, ma_r, mb_s, mb_r, sw_s, sw_r, an_s, an_r,
-    po_s, po_r, id_s, id_r, ta_s, ta_r, ready,
+    po_s, po_r, id_s, id_r, ta_s, ta_r, fa_s, fa_r, ready,
 ):
     me_o = lax.axis_index("owner")
     me_s = lax.axis_index("split")
@@ -296,12 +304,8 @@
             device_id=device, device_id_type=MESH,
         )
 
-    clu_in = pltpu.make_async_copy(clu_hbm, clu_v, in_sem.at[0])
-    emb_in = pltpu.make_async_copy(emb_hbm, emb, in_sem.at[1])
-    ord_in = pltpu.make_async_copy(ord_hbm, ord_v, in_sem.at[2])
-    clu_in.start()
+    emb_in = pltpu.make_async_copy(emb_hbm, emb, in_sem)
     emb_in.start()
-    ord_in.start()
 
     barrier = pltpu.get_barrier_semaphore()
     for k in SPLITS:
@@ -315,8 +319,7 @@
     weave = ones_where(col == ((row >> 1) & 7) * PAIR + (row & 1) * NS + (row >> 4))
     unweave = ones_where(row == ((col >> 1) & 7) * PAIR + (col & 1) * NS + (col >> 4))
 
-    clu_in.wait()
-    clu = clu_v[...]
+    clu = clu_ref[...]
     to_o = clu & (NO - 1)
     to_s = (clu >> 4) & (NS - 1)
     rel_y = ((to_o >> 2) - y) & (NY - 1)
@@ -393,16 +396,8 @@
             tail_out.at[part], keys.at[goal], ta_s, ta_r, (owner_at(k // NC), split_at(k % NC * NZ))
         ).start()
 
-    fill(0)
-    for b in STEPS[0:4]:
-        if b:
-            pl.semaphore_wait(ready.at[b], 1)
-        for k in SPLITS:
-            ship(b, k)
-
     onehot[...] = ones_where(k_o * NZ + rel_z == iota((CHIPS, ROWS), 0))
-    ord_in.wait()
-    orders = ord_v[...]
+    orders = ord_ref[...]
     code = clu + 1
     parts = jnp.where(
         line == 0, orders >> 12,
@@ -427,21 +422,23 @@
             remote(meta_out.at[k], meta_mid.at[k], ma_s, ma_r, (me_o, split_at(k))).start()
     meta_mid[0] = meta_out[0]
 
+    fill(0)
+    for b in STEPS[0:4]:
+        if b:
+            pl.semaphore_wait(ready.at[b], 1)
+        for k in SPLITS:
+            ship(b, k)
+
     fill(4)
+    for b in STEPS[4:FIRST]:
+        pl.semaphore_wait(ready.at[b], 1)
+        for k in SPLITS:
+            ship(b, k)
     fill(8)
     fill(12)
-    for b in STEPS[4:]:
+    for b in STEPS[FIRST:]:
         pl.semaphore_wait(ready.at[b], 1)
-    for b in STEPS[4:FIRST]:
-        for k in SPLITS:
-            ship(b, k)
-
-    some = remote(meta_out.at[pl.ds(1, NS - 1)], meta_mid.at[pl.ds(1, NS - 1)], ma_s, ma_r, (me_o, split_at(1)))
-    some.wait_recv()
-    for k in STEPS[1:]:
-        remote(meta_mid, meta_in.at[k], mb_s, mb_r, (owner_at(k), me_s)).start()
-    meta_in[0] = meta_mid[...]
-    some.wait_send()
+
     wide, thin = pl.ds(POOL, POOLED - POOL), pl.ds(1, NZ - 1)
     pools = remote(pool_out.at[wide], pool_in.at[wide], po_s, po_r, (me_o, split_at(1)))
     names = remote(id_out.at[thin], id_in.at[thin], id_s, id_r, (me_o, split_at(1)))
@@ -457,12 +454,21 @@
     choose = ones_where(ids == iota((BLOCKS * TAIL, POOLED), 0))
     pools.wait_recv()
     tail_out[...] = dot(choose, pool_in[...], (1, 0)).astype(BF16)
+
+    some = remote(meta_out.at[pl.ds(1, NS - 1)], meta_mid.at[pl.ds(1, NS - 1)], ma_s, ma_r, (me_o, split_at(1)))
+    some.wait_recv()
+    for k in STEPS[1:]:
+        remote(meta_mid, meta_in.at[k], mb_s, mb_r, (owner_at(k), me_s)).start()
+    meta_in[0] = meta_mid[...]
+    some.wait_send()
     rest = [(b, k) for b in STEPS[FIRST:] for k in SPLITS]
     blocks = [b * NC + kc for b in STEPS for kc in range(NC)]
     for n, k in enumerate(blocks):
         ship_tail(k)
-        for pair in rest[n * len(rest) // BLOCKS : (n + 1) * len(rest) // BLOCKS]:
+        for pair in rest[n * 3 : (n + 1) * 3]:
             ship(*pair)
+    for pair in rest[BLOCKS * 3 :]:
+        ship(*pair)
 
     many = remote(meta_in.at[pl.ds(1, NO - 1)], meta_in.at[pl.ds(1, NO - 1)], mb_s, mb_r, (owner_at(1), me_s))
     many.wait_recv()
@@ -548,11 +554,21 @@
         best_col[b * NZ : (b + 1) * NZ] = stay
     swap = remote(swap_out, swap_in, sw_s, sw_r, (me_o, split_at(NZ)))
     swap.start()
+    for n, k in enumerate(FAR):
+        far_out[n] = best_col[k : k + 1]
+        far_out[len(FAR) + n] = swap_out[k : k + 1]
+    for n, k in enumerate(FAR):
+        ko, dz = k // NZ, k % NZ
+        remote(
+            far_out.at[n], ans_in.at[k], fa_s, an_r, (owner_at(ko, -1), split_at(dz, -1))
+        ).start()
+        remote(
+            far_out.at[len(FAR) + n], far_in.at[n], fa_s, fa_r, (owner_at(ko, -1), split_at(NZ + dz, -1))
+        ).start()
     swap.wait_recv()
     both = best_col[0:CHIPS] + swap_in[...]
     ans_out[...] = both.reshape(CHIPS, 1, 128)
-    ways = sorted(range(1, CHIPS), key=lambda k: -distance(k // NZ) - min(k % NZ, NZ - k % NZ))
-    for k in ways:
+    for k in WAYS[len(FAR) :]:
         remote(
             ans_out.at[k], ans_in.at[k], an_s, an_r, (owner_at(k // NZ, -1), split_at(k % NZ, -1))
         ).start()
@@ -567,9 +583,14 @@
         remote(
             send.at[span], recv.at[span], send_sem.at[b], recv_sem.at[b], (me_o, split_at(1))
         ).wait_send()
-    most = pl.ds(1, CHIPS - 1)
-    answers = remote(ans_out.at[most], ans_in.at[most], an_s, an_r, (me_o, split_at(1)))
-    answers.wait_recv()
+    most, less = pl.ds(1, CHIPS - 1), pl.ds(1, CHIPS - 1 - len(FAR))
+    remote(ans_out.at[less], ans_in.at[less], an_s, an_r, (me_o, split_at(1))).wait_send()
+    alone = pl.ds(0, len(FAR))
+    remote(far_out, far_out, fa_s, fa_r, (me_o, split_at(1))).wait_send()
+    remote(ans_out.at[most], ans_in.at[most], an_s, an_r, (me_o, split_at(1))).wait_recv()
+    remote(far_out.at[alone], far_in.at[alone], fa_s, fa_r, (me_o, split_at(1))).wait_recv()
+    for n, k in enumerate(FAR):
+        ans_in[k] = ans_in[k] + far_in[n]
 
     table = ans_in[...].reshape(CHIPS, 128).T[0:8]
     high = table.astype(BF16)
@@ -579,14 +600,10 @@
     mine = dot(high, onehot[...], (1, 0)) + dot(mid, onehot[...], (1, 0)) + dot(tiny, onehot[...], (1, 0))
     mine = jnp.sum(jnp.where(line == rel_c * CAP + rank, mine, 0.0), axis=0, keepdims=True)
     out_ref[...] = jnp.where(widest >= FLAG, REDO, mine)
-    answers.wait_send()
 
 
 def common(rows, width):
     return [
-        pltpu.VMEM((ROWS, DIM), BF16),
-        pltpu.VMEM((1, ROWS), jnp.int32),
-        pltpu.VMEM((1, ROWS), jnp.int32),
         pltpu.VMEM((CHIPS, ROWS), BF16),
         pltpu.VMEM((1, ROWS), jnp.int32),
         pltpu.VMEM((rows, width), BF16),
@@ -605,15 +622,15 @@
     ]
 
 
-def call(kernel, name, number, outs, scratch, args):
+def call(kernel, name, number, out, small, scratch, args):
     hbm = pl.BlockSpec(memory_space=pltpu.HBM)
     vmem = pl.BlockSpec(memory_space=pltpu.VMEM)
     return pl.pallas_call(
         kernel,
         name=name,
-        out_shape=outs,
-        in_specs=[hbm] * 3,
-        out_specs=[vmem] * len(outs),
+        out_shape=out,
+        in_specs=[hbm] + [vmem if small else hbm] * 2,
+        out_specs=vmem,
         scratch_shapes=scratch,
         compiler_params=pltpu.CompilerParams(
             collective_id=number, has_side_effects=True, vmem_limit_bytes=56 << 20
@@ -629,7 +646,7 @@
     dma = pltpu.SemaphoreType.DMA
     ready = pltpu.SemaphoreType.REGULAR((NO,))
     result = jax.ShapeDtypeStruct((1, ROWS), F32)
-    pooled_scratch = common(NO * BLOCK, EIGHTH) + [
+    pooled_scratch = [pltpu.VMEM((ROWS, DIM), BF16)] + common(NO * BLOCK, EIGHTH) + [
         pltpu.VMEM((POOLED, DIM), BF16),
         pltpu.VMEM((POOLED, DIM), BF16),
         pltpu.VMEM((NZ, 1, 128), F32),
@@ -637,19 +654,22 @@
         pltpu.VMEM((BLOCKS * TAIL, DIM), BF16),
         pltpu.VMEM((SLOTS, 128), F32),
         pltpu.VMEM((SLOTS, 128), F32),
-        dma((3,)), dma((NO,)), dma((NO,)),
-        *[dma] * 14,
+        pltpu.VMEM((2 * len(FAR), 1, 128), F32),
+        pltpu.VMEM((len(FAR), 1, 128), F32),
+        dma, dma((NO,)), dma((NO,)),
+        *[dma] * 16,
         ready,
     ]
-    full_scratch = common(NO * BLOCK, QUART) + [
+    line = pltpu.VMEM((1, ROWS), jnp.int32)
+    full_scratch = [pltpu.VMEM((ROWS, DIM), BF16), line, line] + common(NO * BLOCK, QUART) + [
         dma((3,)), dma((NO,)), dma((NO,)),
         *[dma] * 8,
         ready,
     ]
-    best = call(pooled_kernel, "pooled", 0, [result], pooled_scratch, args)[0]
+    best = call(pooled_kernel, "pooled", 0, result, True, pooled_scratch, args)
 
     def again(args, best):
-        return call(full_kernel, "full", 1, [result], full_scratch, args)[0]
+        return call(full_kernel, "full", 1, result, False, full_scratch, args)
 
     def keep(args, best):
         return best

time: 67.2 us -> 65.2 us (0.970)
  Pallas kernels: 64.4 us -> 62.4 us
    pallas_call x1, Pallas kernels: 64.4 us -> 62.4 us  [call(): pl.pallas_call(kernel, name=name, out_shape=out, in_specs=[hbm] + [vmem i...]
where the time goes in v4:
time: 65.2 us; the launch traced here: 65.1 us
  Pallas kernels  62.4 us (96%)
  local copies, waits for them, and re-layouts  1.79 us (3%)
  between operations  0.68 us (1%)
    pallas_call x1, Pallas kernels, call(): pl.pallas_call(kernel, name=name, out_shape=out, in_specs=[hbm] + [vmem i...  62.4 us

profile of v4, /device:TPU:1, one launch (start us, length us, event | category | flops | bytes accessed | tf_op | source)
XLA Modules:
  0.0 65.1 jit_solution(7231178709093202103)
XLA Ops:
  0.0 0.0 copy-start.2
  0.0 0.0 copy-start.1
  0.0 0.7 %copy-done.2 = s32[512]{0:T(512)S(1)} copy-done((s32[512]{0:T(512)S(1)}, s32[512]{0:T(512)}, u32[]{:S(2)}) %copy-start.2) | copy-done | bytes 2072
  0.7 0.0 copy-done.1
  0.7 0.0 copy-start
  0.7 62.4 %pooled.1 = f32[1,512]{1,0:T(1,128)S(1)} custom-call(bf16[512,1024]{1,0:T(8,128)(2,1)} %emb_hbm.1, s32[1,512]{1,0:T(1,128)S(1)} %bitcast.7, s32[1,512]{1,0:T(1,128)S(1)} %bitcast.9), custom_call_target="tpu_custom_call" | custom-call | flops 8589934592 | bytes 4194304 | tf_op jit(solution)/shard_map/pooled/pallas_call | solution.py:628
  63.1 0.5 slice.3
  64.3 0.0 copy-done
  64.3 0.2 conditional.1
  64.5 0.6 copy.10
Async XLA Ops:
  0.0 0.7 %copy-start.2 = (s32[512]{0:T(512)S(1)}, s32[512]{0:T(512)}, u32[]{:S(2)}) copy-start(s32[512]{0:T(512)} %param.7) | copy-start | bytes 6148
  0.0 0.7 %copy-start.1 = (s32[512]{0:T(512)S(1)}, s32[512]{0:T(512)}, u32[]{:S(2)}) copy-start(s32[512]{0:T(512)} %param.6) | copy-start | bytes 6148
  0.7 63.6 %copy-start = (bf16[512,1024]{1,0:T(8,128)(2,1)S(1)}, bf16[512,1024]{1,0:T(8,128)(2,1)}, u32[]{:S(2)}) copy-start(bf16[512,1024]{1,0:T(8,128)(2,1)} %emb_hbm.1) | copy-start | bytes 3145732

commit v5 on v4

--- a/solution.py
+++ b/solution.py
@@ -315,9 +315,6 @@
         pl.semaphore_signal(barrier, inc=1, device_id=(owner_at(k), me_s), device_id_type=MESH)
 
     before = ones_where(iota((ROWS, ROWS), 0) < iota((ROWS, ROWS), 1))
-    row, col = iota((BLOCK, BLOCK), 0), iota((BLOCK, BLOCK), 1)
-    weave = ones_where(col == ((row >> 1) & 7) * PAIR + (row & 1) * NS + (row >> 4))
-    unweave = ones_where(row == ((col >> 1) & 7) * PAIR + (col & 1) * NS + (col >> 4))
 
     clu = clu_ref[...]
     to_o = clu & (NO - 1)
@@ -365,6 +362,10 @@
         pl.semaphore_signal(ready.at[k], inc=1, device_id=(owner_at(k, -1), me_s), device_id_type=MESH)
     pool_in[0:POOL] = pool_out[0:POOL]
     id_in[0] = id_out[0]
+
+    row, col = iota((BLOCK, BLOCK), 0), iota((BLOCK, BLOCK), 1)
+    weave = ones_where(col == ((row >> 1) & 7) * PAIR + (row & 1) * NS + (row >> 4))
+    unweave = ones_where(row == ((col >> 1) & 7) * PAIR + (col & 1) * NS + (col >> 4))
 
     def fill(first):
         steps = STEPS[first : first + 4]

time: 65.2 us -> 65.2 us (level)
  no operation moved by 1% of the time
where the time goes in v5:
time: 65.2 us; the launch traced here: 65.1 us
  Pallas kernels  62.4 us (96%)
  local copies, waits for them, and re-layouts  1.79 us (3%)
  between operations  0.68 us (1%)
    pallas_call x1, Pallas kernels, call(): pl.pallas_call(kernel, name=name, out_shape=out, in_specs=[hbm] + [vmem i...  62.4 us

profile of v5, /device:TPU:1, one launch (start us, length us, event | category | flops | bytes accessed | tf_op | source)
XLA Modules:
  0.0 65.1 jit_solution(7787564476201886141)
XLA Ops:
  0.0 0.0 copy-start.2
  0.0 0.0 copy-start.1
  0.0 0.7 %copy-done.2 = s32[512]{0:T(512)S(1)} copy-done((s32[512]{0:T(512)S(1)}, s32[512]{0:T(512)}, u32[]{:S(2)}) %copy-start.2) | copy-done | bytes 2072
  0.7 0.0 copy-done.1
  0.7 0.0 copy-start
  0.7 62.4 %pooled.1 = f32[1,512]{1,0:T(1,128)S(1)} custom-call(bf16[512,1024]{1,0:T(8,128)(2,1)} %emb_hbm.1, s32[1,512]{1,0:T(1,128)S(1)} %bitcast.7, s32[1,512]{1,0:T(1,128)S(1)} %bitcast.9), custom_call_target="tpu_custom_call" | custom-call | flops 8589934592 | bytes 4194304 | tf_op jit(solution)/shard_map/pooled/pallas_call | solution.py:629
  63.1 0.5 slice.3
  64.3 0.0 copy-done
  64.3 0.2 conditional.1
  64.5 0.6 copy.10
Async XLA Ops:
  0.0 0.7 %copy-start.2 = (s32[512]{0:T(512)S(1)}, s32[512]{0:T(512)}, u32[]{:S(2)}) copy-start(s32[512]{0:T(512)} %param.7) | copy-start | bytes 6148
  0.0 0.7 %copy-start.1 = (s32[512]{0:T(512)S(1)}, s32[512]{0:T(512)}, u32[]{:S(2)}) copy-start(s32[512]{0:T(512)} %param.6) | copy-start | bytes 6148
  0.7 63.6 %copy-start = (bf16[512,1024]{1,0:T(8,128)(2,1)S(1)}, bf16[512,1024]{1,0:T(8,128)(2,1)}, u32[]{:S(2)}) copy-start(bf16[512,1024]{1,0:T(8,128)(2,1)} %emb_hbm.1) | copy-start | bytes 3145732
